TPU v7x, 256 devices: a whole 4x4x8 slice. The times are simulated.
256 devices in a mesh: grp: 8 (over y, z_hi), ep: 32 (over x, z_lo, core).
Axes of the slice: x: 4, y: 4, z: 8 (z_hi: 2, z_lo: 4; z = z_hi * 4 + z_lo), core: 2. Of those that a mesh axis runs over, the one named last changes fastest.
Arguments:
- tokens: bfloat16 [4096, 5120], P('ep', 'grp'), may hold values from -6 to 6
- out_grad: bfloat16 [4096, 5120], P('ep', 'grp'), may hold values from -1.5 to 1.5
- expert_ids: int32 [4096, 6], P('ep'), may hold values from 0 to 23, all different within a row; in each aligned block of 128 rows (0 to 127, 128 to 255, ...) at most 40 rows name the same one
- route_probs: bfloat16 [4096, 6], P('ep'), may hold values from 0.049804688 to 0.59765625
- slot_expert: int32 [32], replicated, may hold values from 0 to 23, as said below
- w_gate: bfloat16 [32, 5120, 1024], P('ep', 'grp'), as said below
- w_up: bfloat16 [32, 5120, 1024], P('ep', 'grp'), as said below
- w_down: bfloat16 [32, 5120, 1024], P('ep', 'grp'), as said below
Outputs:
- in_grad: bfloat16 [4096, 5120], P('ep', 'grp')
- grad_gate: bfloat16 [32, 5120, 1024], P('ep', 'grp')
- grad_up: bfloat16 [32, 5120, 1024], P('ep', 'grp')
- grad_down: bfloat16 [32, 5120, 1024], P('ep', 'grp')
Inputs may be any that keep to these rules, and one draw needn't show every extreme that they name: `expert_ids`: in the rows of one index of ep, no expert is named by more than 40 tokens; some expert is named by exactly 40 in some block. `slot_expert`: every expert 0 to 23 is held by at least one of the 32 slots. `w_gate`: slots that hold the same expert hold equal weights. `w_up`: slots that hold the same expert hold equal weights. `w_down`: slots that hold the same expert hold equal weights.
All inputs are finite; a program needn't handle non-finite values.
Results may differ from a plain program's by a relative error of at most 0.03.
Values may be sent and summed in bfloat16 or wider, within the bound.
No kernel may reach another device: no remote copies, remote signals or barrier semaphores. Data moves between devices by JAX's collectives and lax.ppermute only.
A program may use at most 128 MiB of HBM per device.

v0:
```python
import jax
import jax.numpy as jnp
from jax import lax
from jax.sharding import PartitionSpec as P


def activate(gate, up_sum, grad_hidden):
    sigma = jax.nn.sigmoid(gate)
    swish = gate * sigma
    hidden = (swish * up_sum).astype(jnp.bfloat16)
    grad_up = (grad_hidden * swish).astype(jnp.bfloat16)
    grad_gate = (grad_hidden * up_sum * sigma * (1.0 + gate * (1.0 - sigma))).astype(jnp.bfloat16)
    return (hidden, grad_gate, grad_up)


def per_device(tokens, out_grad, expert_ids, route_probs, slot_expert, w_gate, w_up, w_down):
    tok_count, width_part = tokens.shape
    top_count = expert_ids.shape[1]
    num_slots = lax.axis_size("ep")
    in_flight = 3 * num_slots // 4
    capacity = (30 * tok_count + 4 * in_flight - 1) // (4 * in_flight)
    slot_rows = num_slots * capacity
    slot_ids = jnp.arange(num_slots, dtype=jnp.int32)
    same_expert = (slot_expert[:, None] == slot_expert[None, :]).astype(jnp.int32)
    earlier = (slot_ids[:, None] > slot_ids[None, :]).astype(jnp.int32)
    replica_rank = jnp.sum(same_expert * earlier, axis=1)
    flat_ids = expert_ids.reshape(-1)
    hosting = flat_ids[:, None] == slot_expert[None, :]
    replicas = jnp.sum(hosting.astype(jnp.int32), axis=1)
    replica = lax.axis_index("ep") % replicas
    chosen = (hosting & (replica_rank[None, :] == replica[:, None])).astype(jnp.int32)
    target = jnp.sum(chosen * slot_ids[None, :], axis=1)
    position = jnp.sum((jnp.cumsum(chosen, axis=0) - 1) * chosen, axis=1)
    buffer_index = target * capacity + position
    send_tokens = (
        jnp.zeros((slot_rows, width_part), jnp.bfloat16)
        .at[buffer_index]
        .set(jnp.repeat(tokens, top_count, axis=0))
    )
    send_grads = (
        jnp.zeros((slot_rows, width_part), jnp.bfloat16)
        .at[buffer_index]
        .set(jnp.repeat(out_grad, top_count, axis=0))
    )
    send_probs = jnp.zeros((slot_rows,), jnp.bfloat16).at[buffer_index].set(route_probs.reshape(-1))
    recv_tokens, recv_grads, recv_probs = (
        lax.all_to_all(
            send_tokens.reshape(num_slots, capacity, width_part),
            "ep",
            split_axis=0,
            concat_axis=0,
            tiled=True,
        ),
        lax.all_to_all(
            send_grads.reshape(num_slots, capacity, width_part),
            "ep",
            split_axis=0,
            concat_axis=0,
            tiled=True,
        ),
        lax.all_to_all(
            send_probs.reshape(num_slots, capacity), "ep", split_axis=0, concat_axis=0, tiled=True
        ),
    )
    inputs = recv_tokens.reshape(slot_rows, width_part)
    scaled = (
        recv_probs.reshape(slot_rows, 1).astype(jnp.float32)
        * recv_grads.reshape(slot_rows, width_part)
    ).astype(jnp.bfloat16)
    gate_rows = w_gate[0]
    up_rows = w_up[0]
    down_rows = w_down[0]
    gate_part = jnp.dot(inputs, gate_rows, preferred_element_type=jnp.float32)
    up_part = jnp.dot(inputs, up_rows, preferred_element_type=jnp.float32)
    hidden_part = jnp.dot(scaled, down_rows, preferred_element_type=jnp.float32)
    gate, up_sum, grad_hidden = (
        lax.psum(gate_part.astype(jnp.bfloat16), "grp").astype(jnp.float32),
        lax.psum(up_part.astype(jnp.bfloat16), "grp").astype(jnp.float32),
        lax.psum(hidden_part.astype(jnp.bfloat16), "grp").astype(jnp.float32),
    )
    hidden, grad_gate, grad_up = activate(gate, up_sum, grad_hidden)
    part_gate = jnp.dot(inputs.T, grad_gate, preferred_element_type=jnp.float32).astype(
        jnp.bfloat16
    )
    part_up = jnp.dot(inputs.T, grad_up, preferred_element_type=jnp.float32).astype(jnp.bfloat16)
    part_down = jnp.dot(scaled.T, hidden, preferred_element_type=jnp.float32).astype(jnp.bfloat16)
    row_grad = (
        jnp.dot(grad_gate, gate_rows.T, preferred_element_type=jnp.float32)
        + jnp.dot(grad_up, up_rows.T, preferred_element_type=jnp.float32)
    ).astype(jnp.bfloat16)
    returned = lax.all_to_all(
        row_grad.reshape(num_slots, capacity, width_part),
        "ep",
        split_axis=0,
        concat_axis=0,
        tiled=True,
    )
    gathered = returned.reshape(slot_rows, width_part)[buffer_index]
    in_grad = jnp.sum(
        gathered.astype(jnp.float32).reshape(tok_count, top_count, width_part), axis=1
    ).astype(jnp.bfloat16)
    stacked = jnp.stack([part_gate, part_up, part_down])[None]
    mixing = same_expert.astype(jnp.bfloat16)
    mixed = jnp.einsum(
        "st,tkrh->skrh",
        mixing,
        lax.all_to_all(stacked, "ep", split_axis=2, concat_axis=0, tiled=True),
        preferred_element_type=jnp.float32,
    ).astype(jnp.bfloat16)
    summed = lax.all_to_all(mixed, "ep", split_axis=0, concat_axis=2, tiled=True)
    return (in_grad, summed[:, 0], summed[:, 1], summed[:, 2])


def solution(mesh):
    return jax.shard_map(
        per_device,
        mesh=mesh,
        in_specs=(
            P("ep", "grp"),
            P("ep", "grp"),
            P("ep", None),
            P("ep", None),
            P(),
            P("ep", "grp", None),
            P("ep", "grp", None),
            P("ep", "grp", None),
        ),
        out_specs=(
            P("ep", "grp"),
            P("ep", "grp", None),
            P("ep", "grp", None),
            P("ep", "grp", None),
        ),
        check_vma=False,
    )
```

profile of v0, /device:TPU:1, one launch (start us, length us, event | category | flops | bytes accessed | tf_op | source)
XLA Modules:
  0.0 1098.0 jit_solution(3408724642398284460)
XLA Ops:
  7.2 0.0 copy-start
  7.2 0.9 copy.19
  8.1 0.1 eq.70
  8.2 0.1 eq.81
  8.4 0.9 fusion.40
  9.3 0.7 fusion.37
  10.0 0.1 add_select_fusion.1
  10.1 0.1 add_select_fusion
  10.3 0.8 copy.22
  11.1 0.1 reshape.156
  11.2 0.7 and_convert_fusion
  12.0 1.7 reduce-window.6
  13.7 0.3 slice_reduce_fusion
  14.0 0.8 select_reduce_fusion
  14.8 8.6 scatter_custom_fusion
  23.5 0.7 all_to_all.54
  24.2 10.0 all-to-all-start
  34.2 1.1 broadcast_in_dim.34
  35.3 1.1 reshape.172
  36.4 7.5 scatter_custom_fusion.2
  43.9 0.0 all-to-all-done
  43.9 8.1 all-to-all-start.2
  52.0 0.2 broadcast_in_dim.17
  52.2 1.1 reshape.164
  53.3 7.4 scatter_custom_fusion.1
  60.7 31.3 %all-to-all-done.2 = bf16[32,40,640]{2,1,0:T(8,128)(2,1)} async-done(((bf16[32,40,640]{2,1,0:T(8,128)(2,1)}), bf16[32,40,640]{2,1,0:T(8,128)(2,1)}, u32[]{:S(2)}, u32[]{:S(2)}) %all-to-all-start.2) | async-done | bytes 1638432 | tf_op jit(solution)/shard_map/all_to_all | solution.py:47
  92.1 4.2 all-to-all-start.1
  96.3 0.0 all-reduce.3.cloned.1.call-start
  96.4 0.0 copy-start.10
  96.4 5.3 convolution_convert_fusion
  101.7 5.2 convolution_convert_fusion.1
  106.9 29.8 %all-to-all-done.1 = bf16[32,40,640]{2,1,0:T(8,128)(2,1)S(1)} async-done(((bf16[32,40,640]{2,1,0:T(8,128)(2,1)}), bf16[32,40,640]{2,1,0:T(8,128)(2,1)S(1)}, u32[]{:S(2)}, u32[]{:S(2)}) %all-to-all-start.1) | async-done | bytes 1638432 | tf_op jit(solution)/shard_map/all_to_all | solution.py:54
  136.7 0.3 multiply_convert_fusion
  137.0 1.0 copy-done.9
  138.0 3.7 convolution_convert_fusion.2
  141.7 0.0 all-reduce.3.cloned.1.call-update
  141.7 0.1 convert_reduce_fusion
  141.7 0.1 reshape.142
  141.8 1.6 fusion.12
  143.4 629.0 %all-reduce.3.cloned.1.call-done = (bf16[1280,1024]{1,0:T(8,128)(2,1)}, bf16[1280,1024]{1,0:T(8,128)(2,1)}, bf16[1280,1024]{1,0:T(8,128)(2,1)}) async-done(((bf16[1280,1024]{1,0:T(8,128)(2,1)}, bf16[1280,1024]{1,0:T(8,128)(2,1)}, bf16[1280,1024]{1,0:T(8,128)(2,1)}), (bf16[1280,1024]{1,0:T(8,128)(2,1)}, bf16[1280,1024]{1,0:T(8,128)(2,1)}, bf16[1280,1024]{1,0:T(8,128)(2,1)})) %all-reduce.3.cloned.1.call-update) | async-done | bytes 7864336 | tf_op jit(solution)/shard_map/psum | solution.py:78
  772.4 5.3 fusion.24
  777.7 0.0 copy-done.3
  777.7 3.2 fusion
  781.0 4.6 fusion.23
  785.6 3.3 fusion.22
  788.9 0.5 maximum_bitcast_fusion
  789.4 5.7 copy.24
  795.1 6.4 all-to-all-start.4
  801.6 0.0 copy-start.11
  801.6 4.1 fusion.27
  805.7 3.5 fusion.13
  809.2 109.1 %all-to-all-done.4 = bf16[1,3,640,1024]{3,1,0,2:T(4,128)(2,1)} async-done(((bf16[1,3,640,1024]{3,1,0,2:T(4,128)(2,1)}), bf16[1,3,640,1024]{3,1,0,2:T(4,128)(2,1)}, u32[]{:S(2)}, u32[]{:S(2)}) %all-to-all-start.4) | async-done | bytes 3932192 | tf_op jit(solution)/shard_map/all_to_all | solution.py:107
  918.3 4.8 all-to-all-start.3
  923.2 7.9 fusion.16
  931.1 4.4 copy.27
  935.5 28.0 %all-to-all-done.3 = bf16[32,40,640]{2,1,0:T(8,128)(2,1)S(1)} async-done(((bf16[32,40,640]{2,1,0:T(8,128)(2,1)}), bf16[32,40,640]{2,1,0:T(8,128)(2,1)S(1)}, u32[]{:S(2)}, u32[]{:S(2)}) %all-to-all-start.3) | async-done | bytes 1638432 | tf_op jit(solution)/shard_map/all_to_all | solution.py:91
  963.5 5.7 all-to-all-start.5
  969.2 3.4 gather_fusion
  972.6 2.1 gather.6
  974.7 1.5 reduce_sum.55
  976.2 98.6 %all-to-all-done.5 = bf16[32,3,20,1024]{3,2,1,0:T(8,128)(2,1)} async-done(((bf16[32,3,20,1024]{3,2,1,0:T(8,128)(2,1)}), bf16[32,3,20,1024]{3,2,1,0:T(8,128)(2,1)}, u32[]{:S(2)}, u32[]{:S(2)}) %all-to-all-start.5) | async-done | bytes 3932192 | tf_op jit(solution)/shard_map/all_to_all | solution.py:110
  1074.8 5.2 copy.28
  1080.0 6.9 all_to_all.53
  1086.9 4.1 slice_bitcast_fusion
  (24 shorter events, 0.1 us)
Async XLA Ops:
  7.2 89.2 %copy-start = (bf16[1,640,1024]{2,1,0:T(8,128)(2,1)S(1)}, bf16[1,640,1024]{2,1,0:T(8,128)(2,1)}, u32[]{:S(2)}) copy-start(bf16[1,640,1024]{2,1,0:T(8,128)(2,1)} %param.13) | copy-start | bytes 3932164
  24.2 19.7 %all-to-all-start = ((bf16[32,1,40]{2,1,0:T(2,128)(2,1)}), bf16[32,1,40]{2,1,0:T(2,128)(2,1)S(1)}, u32[]{:S(2)}, u32[]{:S(2)}) async-start(bf16[32,1,40]{2,1,0:T(2,128)(2,1)} %all_to_all.54), calls=%async_computation | async-start | bytes 32768 | tf_op jit(solution)/shard_map/all_to_all | solution.py:61
  36.4 15.6 %copy-start.7 = (bf16[128,640]{1,0:T(8,128)(2,1)S(1)}, bf16[128,640]{1,0:T(8,128)(2,1)}, u32[]{:S(2)}) copy-start(bf16[128,640]{1,0:T(8,128)(2,1)} %param.9) | copy-start | bytes 491524
  43.9 48.2 %all-to-all-start.2 = ((bf16[32,40,640]{2,1,0:T(8,128)(2,1)}), bf16[32,40,640]{2,1,0:T(8,128)(2,1)}, u32[]{:S(2)}, u32[]{:S(2)}) async-start(bf16[32,40,640]{2,1,0:T(8,128)(2,1)} %bitcast.6), calls=%async_computation.2 | async-start | bytes 3276800 | tf_op jit(solution)/shard_map/all_to_all | solution.py:47
  92.1 44.6 %all-to-all-start.1 = ((bf16[32,40,640]{2,1,0:T(8,128)(2,1)}), bf16[32,40,640]{2,1,0:T(8,128)(2,1)S(1)}, u32[]{:S(2)}, u32[]{:S(2)}) async-start(bf16[32,40,640]{2,1,0:T(8,128)(2,1)} %bitcast.88), calls=%async_computation.1 | async-start | bytes 3276800 | tf_op jit(solution)/shard_map/all_to_all | solution.py:54
  96.3 676.1 %all-reduce.3.cloned.1.call-start = ((), (), s32[]{:S(2)}) async-start(), calls=%async_computation.6 | async-start | bytes 15728640 | tf_op jit(solution)/shard_map/psum | solution.py:78
  96.4 5.3 copy-start.10
  136.7 1.3 copy-start.9
  772.4 5.3 copy-start.1
  772.4 5.3 copy-start.2
  772.4 5.3 copy-start.3
  781.0 4.6 copy-start.4
  781.0 4.6 copy-start.6
  795.1 123.2 %all-to-all-start.4 = ((bf16[1,3,640,1024]{3,1,0,2:T(4,128)(2,1)}), bf16[1,3,640,1024]{3,1,0,2:T(4,128)(2,1)}, u32[]{:S(2)}, u32[]{:S(2)}) async-start(bf16[1,3,640,1024]{3,1,0,2:T(4,128)(2,1)} %copy.24), calls=%async_computation.4 | async-start | bytes 10485760 | tf_op jit(solution)/shard_map/all_to_all | solution.py:107
  801.5 4.2 copy-start.5
  801.6 4.2 copy-start.11
  809.2 113.9 %copy-start.8 = (s32[32]{0:T(128)S(1)}, s32[32]{0:T(128)}, u32[]{:S(2)}) copy-start(s32[32]{0:T(128)} %param.12) | copy-start | bytes 388
  918.3 45.2 %all-to-all-start.3 = ((bf16[32,40,640]{2,1,0:T(8,128)(2,1)}), bf16[32,40,640]{2,1,0:T(8,128)(2,1)S(1)}, u32[]{:S(2)}, u32[]{:S(2)}) async-start(bf16[32,40,640]{2,1,0:T(8,128)(2,1)} %bitcast.89), calls=%async_computation.3 | async-start | bytes 3276800 | tf_op jit(solution)/shard_map/all_to_all | solution.py:91
  963.5 111.3 %all-to-all-start.5 = ((bf16[32,3,20,1024]{3,2,1,0:T(8,128)(2,1)}), bf16[32,3,20,1024]{3,2,1,0:T(8,128)(2,1)}, u32[]{:S(2)}, u32[]{:S(2)}) async-start(bf16[32,3,20,1024]{3,2,1,0:T(8,128)(2,1)} %copy.27), calls=%async_computation.5 | async-start | bytes 9437184 | tf_op jit(solution)/shard_map/all_to_all | solution.py:110
Sparse Core Ops, SparseCore 0:
  141.8 630.5 all-reduce.2
where the time goes:
time: 1110 us; the launch traced here: 1100 us
  waiting for transfers between devices  926 us (83%)
  local copies, waits for them, and re-layouts  63 us (6%)
  matrix products  42.9 us (4%)
  starting transfers between devices  39.3 us (4%)
  between operations  14.5 us (1%)
  other arithmetic  12.4 us (1%)
    psum x1, waiting for transfers between devices, per_device(): lax.psum(up_part.astype(jnp.bfloat16), 'grp').astype(jnp.float32)  629 us
    all_to_all x1, waiting for transfers between devices, per_device(): lax.all_to_all(stacked, 'ep', split_axis=2, concat_axis=0, tiled=True)  109 us
    all_to_all x1, waiting for transfers between devices, per_device(): lax.all_to_all(mixed, 'ep', split_axis=0, concat_axis=2, tiled=True)  98.6 us
    all_to_all x1, waiting for transfers between devices, per_device(): lax.all_to_all(send_tokens.reshape(num_slots, capacity, width_part), 'ep'...  31.3 us
    all_to_all x1, waiting for transfers between devices, per_device(): lax.all_to_all(send_grads.reshape(num_slots, capacity, width_part), 'ep',...  29.8 us
    all_to_all x1, waiting for transfers between devices, per_device(): lax.all_to_all(row_grad.reshape(num_slots, capacity, width_part), 'ep', s...  28 us
  transfers between devices with their start and end apart: 7, of which 6 were waited for; matrix products, arithmetic and copies ran while one was open for 5% of the time, Pallas kernels for 0%

commit v1 on v0

--- a/solution.py
+++ b/solution.py
@@ -2,6 +2,8 @@
 import jax.numpy as jnp
 from jax import lax
 from jax.sharding import PartitionSpec as P
+
+report_slabs = lambda z: jnp.sum(lax.all_gather(z, axis_name="grp"), 0)
 
 
 def activate(gate, up_sum, grad_hidden):
@@ -75,7 +77,7 @@
     hidden_part = jnp.dot(scaled, down_rows, preferred_element_type=jnp.float32)
     gate, up_sum, grad_hidden = (
         lax.psum(gate_part.astype(jnp.bfloat16), "grp").astype(jnp.float32),
-        lax.psum(up_part.astype(jnp.bfloat16), "grp").astype(jnp.float32),
+        report_slabs(up_part.astype(jnp.bfloat16)).astype(jnp.float32),
         lax.psum(hidden_part.astype(jnp.bfloat16), "grp").astype(jnp.float32),
     )
     hidden, grad_gate, grad_up = activate(gate, up_sum, grad_hidden)

time: 1110 us -> 1220 us (1.099)
  blocking collectives: 0 us -> 50.6 us
  waiting for transfers between devices: 926 us -> 955 us
  starting transfers between devices: 39.3 us -> 62.3 us
  other arithmetic: 12.4 us -> 25.5 us
    all_gather x0 -> x1, waiting for transfers between devices: none -> 166 us  [report_slabs = lambda z: jnp.sum(lax.all_gather(z, axis_name='grp'), 0)]
    psum x1, waiting for transfers between devices: 629 us -> 508 us  [per_device(): lax.psum(hidden_part.astype(jnp.bfloat16), 'grp').astype(jnp.float32)]
    all_to_all x0 -> x1, blocking collectives: none -> 50.6 us  [per_device(): lax.all_to_all(send_tokens.reshape(num_slots, capacity, width_part), 'ep'...]
    all_to_all x1, starting transfers between devices: 4.23 us -> 41.9 us  [per_device(): lax.all_to_all(send_grads.reshape(num_slots, capacity, width_part), 'ep',...]
    all_to_all x1 -> x0, waiting for transfers between devices: 31.3 us -> none  [per_device(): lax.all_to_all(send_tokens.reshape(num_slots, capacity, width_part), 'ep'...]
    all_to_all x1, waiting for transfers between devices: 29.8 us -> 45.9 us  [per_device(): lax.all_to_all(send_grads.reshape(num_slots, capacity, width_part), 'ep',...]
    reduce_sum x0 -> x1, other arithmetic: none -> 13.4 us  [report_slabs = lambda z: jnp.sum(lax.all_gather(z, axis_name='grp'), 0)]
  transfers between devices with their start and end apart: 7 -> 7, of which waited for: 6 -> 6; matrix products, arithmetic and copies ran while one was open for 5% -> 6% of each run, Pallas kernels for 0% -> 0%
where the time goes in v1:
time: 1220 us; the launch traced here: 1210 us
  waiting for transfers between devices  955 us (78%)
  local copies, waits for them, and re-layouts  64.2 us (5%)
  starting transfers between devices  62.3 us (5%)
  blocking collectives  50.6 us (4%)
  matrix products  35.3 us (3%)
  other arithmetic  25.5 us (2%)
  between operations  14.8 us (1%)
    psum x1, waiting for transfers between devices, per_device(): lax.psum(hidden_part.astype(jnp.bfloat16), 'grp').astype(jnp.float32)  508 us
    all_gather x1, waiting for transfers between devices, report_slabs = lambda z: jnp.sum(lax.all_gather(z, axis_name='grp'), 0)  166 us
    all_to_all x1, waiting for transfers between devices, per_device(): lax.all_to_all(stacked, 'ep', split_axis=2, concat_axis=0, tiled=True)  109 us
    all_to_all x1, waiting for transfers between devices, per_device(): lax.all_to_all(mixed, 'ep', split_axis=0, concat_axis=2, tiled=True)  98.6 us
    all_to_all x1, blocking collectives, per_device(): lax.all_to_all(send_tokens.reshape(num_slots, capacity, width_part), 'ep'...  50.6 us
    all_to_all x1, waiting for transfers between devices, per_device(): lax.all_to_all(send_grads.reshape(num_slots, capacity, width_part), 'ep',...  45.9 us
    all_to_all x1, starting transfers between devices, per_device(): lax.all_to_all(send_grads.reshape(num_slots, capacity, width_part), 'ep',...  41.9 us
    all_to_all x1, waiting for transfers between devices, per_device(): lax.all_to_all(row_grad.reshape(num_slots, capacity, width_part), 'ep', s...  28 us
  transfers between devices with their start and end apart: 7, of which 6 were waited for; matrix products, arithmetic and copies ran while one was open for 6% of the time, Pallas kernels for 0%

profile of v1, /device:TPU:1, one launch (start us, length us, event | category | flops | bytes accessed | tf_op | source)
XLA Modules:
  0.0 1207.5 jit_solution(3428191825310815043)
XLA Ops:
  7.2 0.0 all-gather.3.cloned.1.call-start
  7.2 0.9 copy.19
  8.1 0.1 eq.70
  8.3 0.1 eq.81
  8.4 0.9 fusion.40
  9.3 0.7 fusion.37
  10.1 0.1 add_select_fusion.1
  10.2 0.1 add_select_fusion
  10.3 0.7 and_convert_fusion
  11.1 1.7 reduce-window.6
  12.8 0.3 slice_reduce_fusion
  13.1 0.8 select_reduce_fusion
  13.9 1.1 broadcast_in_dim.34
  15.0 1.1 reshape.172
  16.1 6.6 scatter_custom_fusion.2
  22.8 50.6 %all_to_all.61 = bf16[32,40,640]{2,1,0:T(8,128)(2,1)S(1)} all-to-all(bf16[32,40,640]{2,1,0:T(8,128)(2,1)S(1)} %bitcast.91), channel_id=1, replica_groups=mesh['grp'=8,'ep'=32] {'ep'}, dimensions={0} | all-to-all | bytes 3276800 | tf_op jit(solution)/shard_map/all_to_all | solution.py:49
  73.4 1.2 copy-done.7
  74.6 3.7 convolution_convert_fusion.1
  78.3 0.7 copy-done.13
  78.9 0.1 copy.22
  79.1 0.2 reshape.156
  79.2 8.6 scatter_custom_fusion
  87.8 0.7 all_to_all.54
  88.6 4.2 all-to-all-start
  92.8 0.2 broadcast_in_dim.17
  92.9 1.1 reshape.164
  94.1 7.6 scatter_custom_fusion.1
  101.7 41.9 %all-to-all-start.1 = ((bf16[32,40,640]{2,1,0:T(8,128)(2,1)}), bf16[32,40,640]{2,1,0:T(8,128)(2,1)S(1)}, u32[]{:S(2)}, u32[]{:S(2)}) async-start(bf16[32,40,640]{2,1,0:T(8,128)(2,1)} %bitcast.90), calls=%async_computation.1 | async-start | bytes 3276800 | tf_op jit(solution)/shard_map/all_to_all | solution.py:56
  143.6 0.0 all-reduce.3.cloned.1.call-start
  143.7 45.9 %all-to-all-done.1 = bf16[32,40,640]{2,1,0:T(8,128)(2,1)S(1)} async-done(((bf16[32,40,640]{2,1,0:T(8,128)(2,1)}), bf16[32,40,640]{2,1,0:T(8,128)(2,1)S(1)}, u32[]{:S(2)}, u32[]{:S(2)}) %all-to-all-start.1) | async-done | bytes 1638432 | tf_op jit(solution)/shard_map/all_to_all | solution.py:56
  189.5 0.3 multiply_convert_fusion
  189.9 1.2 copy-done.8
  191.1 3.7 convolution_convert_fusion
  194.8 3.8 convolution_convert_fusion.2
  198.6 0.1 convert_reduce_fusion
  198.7 0.1 reshape.142
  198.8 1.5 fusion.12
  200.3 165.5 %all-gather.3.cloned.1.call-done = bf16[10240,1024]{1,0:T(8,128)(2,1)} async-done(((bf16[1280,1024]{1,0:T(8,128)(2,1)}), bf16[10240,1024]{1,0:T(8,128)(2,1)}) %all-gather.3.cloned.1.call-update) | async-done | bytes 20971536 | tf_op jit(solution)/shard_map/all_gather | solution.py:6
  365.8 13.4 %reduce_sum.67 = bf16[1280,1024]{1,0:T(8,128)(2,1)} reduce(bf16[8,1280,1024]{2,1,0:T(8,128)(2,1)} %bitcast.89, bf16[]{:T(256)} %constant.11.clone.1), dimensions={0}, to_apply=%region_10.11 | reduce | flops 9175040 | bytes 23592962 | tf_op jit(solution)/shard_map/reduce_sum | solution.py:6
  379.2 507.5 %all-reduce.3.cloned.1.call-done = (bf16[1280,1024]{1,0:T(8,128)(2,1)}, bf16[1280,1024]{1,0:T(8,128)(2,1)}) async-done(((bf16[1280,1024]{1,0:T(8,128)(2,1)}, bf16[1280,1024]{1,0:T(8,128)(2,1)}), (bf16[1280,1024]{1,0:T(8,128)(2,1)}, bf16[1280,1024]{1,0:T(8,128)(2,1)})) %all-reduce.3.cloned.1.call-update) | async-done | bytes 5242896 | tf_op jit(solution)/shard_map/psum | solution.py:81
  886.7 4.8 fusion.24
  891.6 0.0 copy-done.3
  891.6 3.0 fusion
  894.6 1.9 fusion.23
  896.6 0.4 copy-done.6
  897.0 1.9 fusion.22
  898.9 0.5 maximum_bitcast_fusion
  899.4 5.7 copy.24
  905.1 5.7 all-to-all-start.4
  910.9 4.1 fusion.27
  915.0 3.5 fusion.13
  918.5 109.2 %all-to-all-done.4 = bf16[1,3,640,1024]{3,1,0,2:T(4,128)(2,1)} async-done(((bf16[1,3,640,1024]{3,1,0,2:T(4,128)(2,1)}), bf16[1,3,640,1024]{3,1,0,2:T(4,128)(2,1)}, u32[]{:S(2)}, u32[]{:S(2)}) %all-to-all-start.4) | async-done | bytes 3932192 | tf_op jit(solution)/shard_map/all_to_all | solution.py:109
  1027.7 4.9 all-to-all-start.3
  1032.6 7.9 fusion.16
  1040.5 4.4 copy.27
  1044.9 28.0 %all-to-all-done.3 = bf16[32,40,640]{2,1,0:T(8,128)(2,1)S(1)} async-done(((bf16[32,40,640]{2,1,0:T(8,128)(2,1)}), bf16[32,40,640]{2,1,0:T(8,128)(2,1)S(1)}, u32[]{:S(2)}, u32[]{:S(2)}) %all-to-all-start.3) | async-done | bytes 1638432 | tf_op jit(solution)/shard_map/all_to_all | solution.py:93
  1072.9 5.5 all-to-all-start.5
  1078.4 3.4 gather_fusion
  1081.8 2.1 gather.6
  1083.9 1.5 reduce_sum.68
  1085.4 98.6 %all-to-all-done.5 = bf16[32,3,20,1024]{3,2,1,0:T(8,128)(2,1)} async-done(((bf16[32,3,20,1024]{3,2,1,0:T(8,128)(2,1)}), bf16[32,3,20,1024]{3,2,1,0:T(8,128)(2,1)}, u32[]{:S(2)}, u32[]{:S(2)}) %all-to-all-start.5) | async-done | bytes 3932192 | tf_op jit(solution)/shard_map/all_to_all | solution.py:112
  1184.0 5.2 copy.28
  1189.2 6.9 all_to_all.53
  1196.1 4.1 slice_bitcast_fusion
  (37 shorter events, 0.2 us)
Async XLA Ops:
  7.2 182.7 %copy-start = (bf16[1,640,1024]{2,1,0:T(8,128)(2,1)S(1)}, bf16[1,640,1024]{2,1,0:T(8,128)(2,1)}, u32[]{:S(2)}) copy-start(bf16[1,640,1024]{2,1,0:T(8,128)(2,1)} %param.13) | copy-start | bytes 3932164
  7.2 358.6 %all-gather.3.cloned.1.call-start = ((), (), s32[]{:S(2)}) async-start(), calls=%async_computation.6 | async-start | bytes 23592960 | tf_op jit(solution)/shard_map/all_gather | solution.py:6
  22.7 51.8 %copy-start.15 = (bf16[1,640,1024]{2,1,0:T(8,128)(2,1)S(1)}, bf16[1,640,1024]{2,1,0:T(8,128)(2,1)}, u32[]{:S(2)}) copy-start(bf16[1,640,1024]{2,1,0:T(8,128)(2,1)} %param.14) | copy-start | bytes 3932164
  73.4 1.2 copy-start.7
  78.2 0.7 copy-start.13
  78.2 14.5 %copy-start.11 = (bf16[128,640]{1,0:T(8,128)(2,1)S(1)}, bf16[128,640]{1,0:T(8,128)(2,1)}, u32[]{:S(2)}) copy-start(bf16[128,640]{1,0:T(8,128)(2,1)} %param.9) | copy-start | bytes 491524
  88.6 13.1 %all-to-all-start = ((bf16[32,1,40]{2,1,0:T(2,128)(2,1)}), bf16[32,1,40]{2,1,0:T(2,128)(2,1)S(1)}, u32[]{:S(2)}, u32[]{:S(2)}) async-start(bf16[32,1,40]{2,1,0:T(2,128)(2,1)} %all_to_all.54), calls=%async_computation | async-start | bytes 32768 | tf_op jit(solution)/shard_map/all_to_all | solution.py:63
  101.7 87.9 %all-to-all-start.1 = ((bf16[32,40,640]{2,1,0:T(8,128)(2,1)}), bf16[32,40,640]{2,1,0:T(8,128)(2,1)S(1)}, u32[]{:S(2)}, u32[]{:S(2)}) async-start(bf16[32,40,640]{2,1,0:T(8,128)(2,1)} %bitcast.90), calls=%async_computation.1 | async-start | bytes 3276800 | tf_op jit(solution)/shard_map/all_to_all | solution.py:56
  143.6 743.1 %all-reduce.3.cloned.1.call-start = ((), (), s32[]{:S(2)}) async-start(), calls=%async_computation.7 | async-start | bytes 10485760 | tf_op jit(solution)/shard_map/psum | solution.py:81
  189.5 1.6 copy-start.8
  191.1 3.7 copy-start.14
  365.8 520.9 %copy-start.10 = (bf16[1280,640]{1,0:T(8,128)(2,1)S(1)}, bf16[1280,640]{1,0:T(8,128)(2,1)}, u32[]{:S(2)}) copy-start(bf16[1280,640]{1,0:T(8,128)(2,1)} %fusion.12) | copy-start | bytes 4915204
  886.7 4.8 copy-start.1
  886.7 4.8 copy-start.2
  886.7 4.9 copy-start.3
  891.6 3.0 copy-start.9
  894.6 1.9 copy-start.4
  894.6 2.4 copy-start.6
  905.1 122.6 %all-to-all-start.4 = ((bf16[1,3,640,1024]{3,1,0,2:T(4,128)(2,1)}), bf16[1,3,640,1024]{3,1,0,2:T(4,128)(2,1)}, u32[]{:S(2)}, u32[]{:S(2)}) async-start(bf16[1,3,640,1024]{3,1,0,2:T(4,128)(2,1)} %copy.24), calls=%async_computation.4 | async-start | bytes 10485760 | tf_op jit(solution)/shard_map/all_to_all | solution.py:109
  910.9 4.2 copy-start.5
  910.9 4.2 copy-start.16
  918.5 114.1 %copy-start.12 = (s32[32]{0:T(128)S(1)}, s32[32]{0:T(128)}, u32[]{:S(2)}) copy-start(s32[32]{0:T(128)} %param.12) | copy-start | bytes 388
  1027.7 45.2 %all-to-all-start.3 = ((bf16[32,40,640]{2,1,0:T(8,128)(2,1)}), bf16[32,40,640]{2,1,0:T(8,128)(2,1)S(1)}, u32[]{:S(2)}, u32[]{:S(2)}) async-start(bf16[32,40,640]{2,1,0:T(8,128)(2,1)} %bitcast.96), calls=%async_computation.3 | async-start | bytes 3276800 | tf_op jit(solution)/shard_map/all_to_all | solution.py:93
  1072.9 111.1 %all-to-all-start.5 = ((bf16[32,3,20,1024]{3,2,1,0:T(8,128)(2,1)}), bf16[32,3,20,1024]{3,2,1,0:T(8,128)(2,1)}, u32[]{:S(2)}, u32[]{:S(2)}) async-start(bf16[32,3,20,1024]{3,2,1,0:T(8,128)(2,1)} %copy.27), calls=%async_computation.5 | async-start | bytes 9437184 | tf_op jit(solution)/shard_map/all_to_all | solution.py:112
Sparse Core Ops, SparseCore 0:
  78.4 287.3 all-gather.2
  368.5 518.1 all-reduce.2
